TPU v7x, 32 devices: a whole 2x2x4 slice. The times are simulated.
32 devices in a mesh: dp: 8 (over z, x), tensor: 4 (over y, core).
Axes of the slice: x: 2, y: 2, z: 4, core: 2. Of those that a mesh axis runs over, the one named last changes fastest.
Arguments:
- layer_input: bfloat16 [4096, 768], P('dp', 'tensor'), may hold values from -6 to 6
- segment_ids: int32 [8, 512], P('dp'), may hold values from 0 to 15, never falling along the last dimension, each value on 1 to 256 neighbouring positions
- triple_weight: bfloat16 [768, 3, 768], P(None, None, 'tensor'), may hold values from -0.21875 to 0.21875
- query_value_bias: float32 [2, 768], P(None, 'tensor'), may hold values from -3 to 3
- output_weight: bfloat16 [768, 768], P('tensor'), may hold values from -0.875 to 0.875
- output_bias: float32 [768], P('tensor'), may hold values from -3 to 3
- norm_gain: float32 [768], P('tensor'), may hold values from 0.5 to 1.5
- norm_shift: float32 [768], P('tensor'), may hold values from -3 to 3
- expand_weight: bfloat16 [768, 3072], P(None, 'tensor'), may hold values from -0.21875 to 0.21875
- expand_bias: float32 [3072], P('tensor'), may hold values from -3 to 3
- reduce_weight: bfloat16 [3072, 768], P('tensor'), may hold values from -0.109375 to 0.109375
- reduce_bias: float32 [768], P('tensor'), may hold values from -3 to 3
- final_gain: float32 [768], P('tensor'), may hold values from 0.5 to 1.5
- final_shift: float32 [768], P('tensor'), may hold values from -3 to 3
- cotangent: bfloat16 [4096, 768], P('dp', 'tensor'), may hold values from -6 to 6
Outputs:
- layer_output: bfloat16 [4096, 768], P('dp', 'tensor')
- input_grad: float32 [4096, 768], P('dp', 'tensor')
- triple_grad: float32 [768, 3, 768], P(None, None, 'tensor')
- query_value_grad: float32 [2, 768], P(None, 'tensor')
- output_weight_grad: float32 [768, 768], P('tensor')
- output_bias_grad: float32 [768], P('tensor')
- norm_gain_grad: float32 [768], P('tensor')
- norm_shift_grad: float32 [768], P('tensor')
- expand_weight_grad: float32 [768, 3072], P(None, 'tensor')
- expand_bias_grad: float32 [3072], P('tensor')
- reduce_weight_grad: float32 [3072, 768], P('tensor')
- reduce_bias_grad: float32 [768], P('tensor')
- final_gain_grad: float32 [768], P('tensor')
- final_shift_grad: float32 [768], P('tensor')
Inputs may be any that keep to these rules, and one draw needn't show every extreme that they name: `segment_ids`: segment numbers never fall along a sequence; each document holds 1 to 256 tokens.
All inputs are finite; a program needn't handle non-finite values.
Results may differ from a plain program's by a relative error of at most 0.012.
The roundings to bfloat16 on the way count: a program that leaves them out, or rounds other values in their place, can miss the bound.
Values may be sent and summed in bfloat16 or wider, within the bound.
A program may use at most 64 MiB of HBM per device.

v0:
```python
import jax
import jax.numpy as jnp
from jax import lax
from jax.sharding import PartitionSpec as P

D = 768
HD = 64
EPS = 1e-06


def gelu_value(pre_act):
    return 0.5 * pre_act * (1.0 + lax.erf(pre_act * 0.7071067811865476))


def gelu_slope(pre_act):
    return (
        0.5 * (1.0 + lax.erf(pre_act * 0.7071067811865476))
        + pre_act * jnp.exp(-0.5 * pre_act * pre_act) * 0.3989422804014327
    )


def widen(piece):
    return lax.all_gather(piece, "tensor", axis=1, tiled=True)


def row_stats(first, second):
    return lax.psum((jnp.sum(first, axis=1), jnp.sum(second, axis=1)), "tensor")


def norm_forward(hidden, gain, shift):
    total, squares = row_stats(hidden, hidden * hidden)
    row_mean = (total / D)[:, None]
    inverse = lax.rsqrt(squares[:, None] / D - row_mean * row_mean + EPS)
    normed = (hidden - row_mean) * inverse
    return (normed * gain + shift, normed, inverse)


def norm_backward(upstream, normed, inverse, gain):
    scaled = upstream * gain
    first_total, second_total = row_stats(scaled, scaled * normed)
    return inverse * (scaled - first_total[:, None] / D - normed * second_total[:, None] / D)


def tall_dot(left, right):
    return lax.dot_general(
        left, right, (((0,), (0,)), ((), ())), preferred_element_type=jnp.float32
    )


def wide_dot(left, right):
    return lax.dot_general(
        left, right, (((1,), (1,)), ((), ())), preferred_element_type=jnp.float32
    )


def masked_scores(query_part, key_part, segment_row, head_scale):
    scores = (
        jnp.einsum("qhd,khd->hqk", query_part, key_part, preferred_element_type=jnp.float32)
        * head_scale
    )
    allowed = segment_row[:, None] == segment_row[None, :]
    return jnp.where(allowed[None], scores, -jnp.inf)


def per_device(
    layer_input,
    segment_ids,
    triple_weight,
    query_value_bias,
    output_weight,
    output_bias,
    norm_gain,
    norm_shift,
    expand_weight,
    expand_bias,
    reduce_weight,
    reduce_bias,
    final_gain,
    final_shift,
    cotangent,
):
    seq_count = segment_ids.shape[0]
    seq_len = segment_ids.shape[1]
    tok_count = seq_count * seq_len
    local_width = triple_weight.shape[2]
    local_heads = local_width // HD
    head_scale = HD ** (-0.5)
    gathered = widen(layer_input)
    projected = jnp.einsum(
        "td,dcf->tcf", gathered, triple_weight, preferred_element_type=jnp.float32
    )
    query_half = (
        (projected[:, 0] + query_value_bias[0])
        .astype(jnp.bfloat16)
        .reshape(seq_count, seq_len, local_heads, HD)
    )
    key_half = projected[:, 1].astype(jnp.bfloat16).reshape(seq_count, seq_len, local_heads, HD)
    value_half = (
        (projected[:, 2] + query_value_bias[1])
        .astype(jnp.bfloat16)
        .reshape(seq_count, seq_len, local_heads, HD)
    )
    seq_index = 0
    scores = masked_scores(
        query_half[seq_index], key_half[seq_index], segment_ids[seq_index], head_scale
    )
    top = jnp.max(scores, axis=-1, keepdims=True)
    log_total = top + jnp.log(jnp.sum(jnp.exp(scores - top), axis=-1, keepdims=True))
    probs_half = jnp.exp(scores - log_total).astype(jnp.bfloat16)
    context_list = [
        jnp.einsum(
            "hqk,khd->qhd", probs_half, value_half[seq_index], preferred_element_type=jnp.float32
        ).astype(jnp.bfloat16)
    ]
    total_list = [log_total]
    context = jnp.stack(context_list)
    context_flat = context.reshape(tok_count, local_width)
    attn_share = lax.psum_scatter(
        jnp.dot(context_flat, output_weight, preferred_element_type=jnp.float32),
        "tensor",
        scatter_dimension=1,
        tiled=True,
    )
    first_sum = layer_input.astype(jnp.float32) + attn_share + output_bias
    attended, normed_one, inv_one = norm_forward(first_sum, norm_gain, norm_shift)
    attended_half = widen(attended.astype(jnp.bfloat16))
    pre_act = (
        jnp.dot(attended_half, expand_weight, preferred_element_type=jnp.float32) + expand_bias
    )
    activated = gelu_value(pre_act).astype(jnp.bfloat16)
    mlp_share = lax.psum_scatter(
        jnp.dot(activated, reduce_weight, preferred_element_type=jnp.float32),
        "tensor",
        scatter_dimension=1,
        tiled=True,
    )
    second_sum = attended + mlp_share + reduce_bias
    out_f, normed_two, inv_two = norm_forward(second_sum, final_gain, final_shift)
    layer_output = out_f.astype(jnp.bfloat16)
    upstream = cotangent.astype(jnp.float32)
    final_gain_grad = jnp.sum(upstream * normed_two, axis=0)
    final_shift_grad = jnp.sum(upstream, axis=0)
    second_grad = norm_backward(upstream, normed_two, inv_two, final_gain)
    second_half = widen(second_grad.astype(jnp.bfloat16))
    reduce_weight_grad = tall_dot(activated, second_half)
    reduce_bias_grad = jnp.sum(second_grad, axis=0)
    act_grad = wide_dot(second_half, reduce_weight) * gelu_slope(pre_act)
    act_half = act_grad.astype(jnp.bfloat16)
    expand_weight_grad = tall_dot(attended_half, act_half)
    expand_bias_grad = jnp.sum(act_grad, axis=0)
    attended_grad = second_grad + lax.psum_scatter(
        wide_dot(act_half, expand_weight), "tensor", scatter_dimension=1, tiled=True
    )
    norm_gain_grad = jnp.sum(attended_grad * normed_one, axis=0)
    norm_shift_grad = jnp.sum(attended_grad, axis=0)
    first_grad = norm_backward(attended_grad, normed_one, inv_one, norm_gain)
    first_half = widen(first_grad.astype(jnp.bfloat16))
    output_weight_grad = tall_dot(context_flat, first_half)
    output_bias_grad = jnp.sum(first_grad, axis=0)
    context_grad = (
        wide_dot(first_half, output_weight)
        .astype(jnp.bfloat16)
        .reshape(seq_count, seq_len, local_heads, HD)
    )
    seq_index = 0
    scores = masked_scores(
        query_half[seq_index], key_half[seq_index], segment_ids[seq_index], head_scale
    )
    probs = jnp.exp(scores - total_list[seq_index])
    probs_half = probs.astype(jnp.bfloat16)
    grad_part = context_grad[seq_index]
    value_list = [
        jnp.einsum("hqk,qhd->khd", probs_half, grad_part, preferred_element_type=jnp.float32)
    ]
    prob_grad = jnp.einsum(
        "qhd,khd->hqk", grad_part, value_half[seq_index], preferred_element_type=jnp.float32
    )
    delta = jnp.einsum(
        "qhd,qhd->hq", grad_part.astype(jnp.float32), context[seq_index].astype(jnp.float32)
    )
    score_grad = (probs * (prob_grad - delta[:, :, None]) * head_scale).astype(jnp.bfloat16)
    query_list = [
        jnp.einsum(
            "hqk,khd->qhd", score_grad, key_half[seq_index], preferred_element_type=jnp.float32
        )
    ]
    key_list = [
        jnp.einsum(
            "hqk,qhd->khd", score_grad, query_half[seq_index], preferred_element_type=jnp.float32
        )
    ]
    query_grad = jnp.stack(query_list).reshape(tok_count, local_width)
    key_grad = jnp.stack(key_list).reshape(tok_count, local_width)
    value_grad = jnp.stack(value_list).reshape(tok_count, local_width)
    query_value_grad = jnp.stack([jnp.sum(query_grad, axis=0), jnp.sum(value_grad, axis=0)])
    triple_half = jnp.stack([query_grad, key_grad, value_grad], axis=1).astype(jnp.bfloat16)
    triple_grad = jnp.einsum(
        "td,tcf->dcf", gathered, triple_half, preferred_element_type=jnp.float32
    )
    input_terms = jnp.einsum(
        "tcf,dcf->td", triple_half, triple_weight, preferred_element_type=jnp.float32
    )
    input_grad = first_grad + lax.psum_scatter(
        input_terms, "tensor", scatter_dimension=1, tiled=True
    )
    (
        triple_grad,
        query_value_grad,
        output_weight_grad,
        output_bias_grad,
        norm_gain_grad,
        norm_shift_grad,
        expand_weight_grad,
        expand_bias_grad,
        reduce_weight_grad,
        reduce_bias_grad,
        final_gain_grad,
        final_shift_grad,
    ) = lax.psum(
        (
            triple_grad,
            query_value_grad,
            output_weight_grad,
            output_bias_grad,
            norm_gain_grad,
            norm_shift_grad,
            expand_weight_grad,
            expand_bias_grad,
            reduce_weight_grad,
            reduce_bias_grad,
            final_gain_grad,
            final_shift_grad,
        ),
        "dp",
    )
    return (
        layer_output,
        input_grad,
        triple_grad,
        query_value_grad,
        output_weight_grad,
        output_bias_grad,
        norm_gain_grad,
        norm_shift_grad,
        expand_weight_grad,
        expand_bias_grad,
        reduce_weight_grad,
        reduce_bias_grad,
        final_gain_grad,
        final_shift_grad,
    )


def solution(mesh):
    in_specs = (
        P("dp", "tensor"),
        P("dp", None),
        P(None, None, "tensor"),
        P(None, "tensor"),
        P("tensor", None),
        P("tensor"),
        P("tensor"),
        P("tensor"),
        P(None, "tensor"),
        P("tensor"),
        P("tensor", None),
        P("tensor"),
        P("tensor"),
        P("tensor"),
        P("dp", "tensor"),
    )
    out_specs = (
        P("dp", "tensor"),
        P("dp", "tensor"),
        P(None, None, "tensor"),
        P(None, "tensor"),
        P("tensor", None),
        P("tensor"),
        P("tensor"),
        P("tensor"),
        P(None, "tensor"),
        P("tensor"),
        P("tensor", None),
        P("tensor"),
        P("tensor"),
        P("tensor"),
    )
    return jax.shard_map(
        per_device, mesh=mesh, in_specs=in_specs, out_specs=out_specs, check_vma=False
    )
```

profile of v0, /device:TPU:0, one launch (start us, length us, event | category | flops | bytes accessed | tf_op | source)
XLA Modules:
  0.0 474.9 jit_solution(481683990149905921)
XLA Ops:
  7.2 10.4 %all_gather.12 = bf16[512,768]{0,1:T(8,128)(2,1)S(1)} all-gather(bf16[512,192]{0,1:T(8,128)(2,1)} %param.15), channel_id=1, replica_groups=mesh['dp'=8,'tensor'=4] {'tensor'}, dimensions={1}, use_global_device_ids=true | all-gather | bytes 983040 | tf_op jit(solution)/shard_map/all_gather | solution.py:23
  17.7 1.8 fusion.41
  19.5 0.8 fusion.33
  20.7 0.8 fusion.1
  21.6 0.7 exponential_reduce_fusion
  22.3 0.9 copy-done.1
  23.2 1.0 convolution_convert_fusion.1
  24.3 1.6 fusion.37
  25.9 29.1 %reduce-scatter.5.cloned.1.call-done = f32[512,192]{0,1:T(8,128)} async-done(((f32[512,768]{0,1:T(8,128)}), f32[512,192]{0,1:T(8,128)}) %reduce-scatter.5.cloned.1.call-update) | async-done | bytes 393232 | tf_op jit(solution)/shard_map/reduce_scatter | solution.py:118
  55.0 1.1 fusion.30
  56.2 5.8 %all-reduce.5 = (f32[512]{0:T(512)S(1)}, f32[512]{0:T(512)S(1)}) all-reduce(f32[512]{0:T(512)S(1)} %get-tuple-element.23, f32[512]{0:T(512)S(1)} %get-tuple-element.22), channel_id=1, replica_groups=mesh['dp'=8,'tensor'=4] {'tensor'}, use_global_device_ids=true, to_apply=%region_6.7 | all-reduce | flops 1024 | bytes 8192 | tf_op jit(solution)/shard_map/psum | solution.py:27
  62.1 8.8 %all_gather.13 = bf16[512,768]{0,1:T(8,128)(2,1)S(1)} all-gather(bf16[512,192]{0,1:T(8,128)(2,1)S(1)} %fusion.20), channel_id=1, replica_groups=mesh['dp'=8,'tensor'=4] {'tensor'}, dimensions={1}, use_global_device_ids=true | all-gather | bytes 983040 | tf_op jit(solution)/shard_map/all_gather | solution.py:23
  70.8 0.9 copy-done.3
  71.7 2.1 multiply_convert_fusion.1
  73.8 0.9 copy-done.19
  74.7 2.0 fusion.38
  76.7 28.3 %reduce-scatter.7.cloned.1.call-done = f32[512,192]{0,1:T(8,128)} async-done(((f32[512,768]{0,1:T(8,128)}), f32[512,192]{0,1:T(8,128)}) %reduce-scatter.7.cloned.1.call-update) | async-done | bytes 393232 | tf_op jit(solution)/shard_map/reduce_scatter | solution.py:131
  105.0 1.2 fusion.29
  106.2 5.8 %all-reduce.4 = (f32[512]{0:T(512)S(1)}, f32[512]{0:T(512)S(1)}) all-reduce(f32[512]{0:T(512)S(1)} %get-tuple-element.21, f32[512]{0:T(512)S(1)} %get-tuple-element.20), channel_id=1, replica_groups=mesh['dp'=8,'tensor'=4] {'tensor'}, use_global_device_ids=true, to_apply=%region_11.12 | all-reduce | flops 1024 | bytes 8192 | tf_op jit(solution)/shard_map/psum | solution.py:27
  112.1 6.2 %all-reduce.3 = (f32[512]{0:T(512)}, f32[512]{0:T(512)S(1)}) all-reduce(f32[512]{0:T(512)S(1)} %get-tuple-element.25, f32[512]{0:T(512)S(1)} %get-tuple-element.24), channel_id=1, replica_groups=mesh['dp'=8,'tensor'=4] {'tensor'}, use_global_device_ids=true, to_apply=%region_15.16 | all-reduce | flops 1024 | bytes 8192 | tf_op jit(solution)/shard_map/psum | solution.py:27
  118.4 0.9 fusion.28
  119.3 8.9 %all_gather.14 = bf16[512,768]{0,1:T(8,128)(2,1)S(1)} all-gather(bf16[512,192]{0,1:T(8,128)(2,1)S(1)} %fusion.28), channel_id=1, replica_groups=mesh['dp'=8,'tensor'=4] {'tensor'}, dimensions={1}, use_global_device_ids=true | all-gather | bytes 983040 | tf_op jit(solution)/shard_map/all_gather | solution.py:23
  128.2 4.3 fusion.36
  132.5 3.1 fusion.18
  135.7 28.7 %reduce-scatter.9.cloned.1.call-done = f32[512,192]{0,1:T(8,128)} async-done(((f32[512,768]{0,1:T(8,128)}), f32[512,192]{0,1:T(8,128)}) %reduce-scatter.9.cloned.1.call-update) | async-done | bytes 393232 | tf_op jit(solution)/shard_map/reduce_scatter | solution.py:151
  164.4 2.7 fusion.14
  167.1 5.7 %all-reduce.2 = (f32[512]{0:T(512)S(1)}, f32[512]{0:T(512)S(1)}) all-reduce(f32[512]{0:T(512)S(1)} %get-tuple-element.58, f32[512]{0:T(512)S(1)} %get-tuple-element.57), channel_id=1, replica_groups=mesh['dp'=8,'tensor'=4] {'tensor'}, use_global_device_ids=true, to_apply=%region_20.21 | all-reduce | flops 1024 | bytes 8192 | tf_op jit(solution)/shard_map/psum | solution.py:27
  172.9 1.4 fusion.31
  174.3 9.1 %all_gather.15 = bf16[512,768]{0,1:T(8,128)(2,1)S(1)} all-gather(bf16[512,192]{0,1:T(8,128)(2,1)S(1)} %convert_element_type.69), channel_id=1, replica_groups=mesh['dp'=8,'tensor'=4] {'tensor'}, dimensions={1}, use_global_device_ids=true | all-gather | bytes 983040 | tf_op jit(solution)/shard_map/all_gather | solution.py:23
  183.4 1.3 convolution_convert_fusion.2
  184.8 1.1 fusion.35
  186.0 1.4 multiply_convert_fusion
  187.4 0.6 convolution_convert_fusion
  188.3 0.5 fusion.34
  188.9 2.0 convolution_bitcast_fusion.1
  191.0 3.7 fusion.16
  194.7 2.2 fusion.40
  197.0 1.2 fusion.39
  198.2 1.9 convolution_bitcast_fusion
  200.3 0.4 copy-done.40
  200.8 37.6 %all-reduce = (f32[2,192]{1,0:T(2,128)}, f32[192]{0:T(256)}, f32[192]{0:T(256)}, f32[192]{0:T(256)}, f32[768]{0:T(1024)}, /*index=5*/f32[192]{0:T(256)}, f32[192]{0:T(256)}, f32[192]{0:T(256)}) all-reduce(f32[2,192]{1,0:T(2,128)S(1)} %pad_maximum_fusion.3, f32[192]{0:T(256)S(1)} %get-tuple-element.49, ...), channel_id=1, replica_groups=mesh['dp'=8,'tensor'=4] {'dp'}, use_global_device_ids=true, to_apply=%region_25.26 | all-reduce | flops 2304 | bytes 18432 | tf_op jit(solution)/shard_map/psum | solution.py:219
  238.4 1.8 add.169
  240.2 220.4 %all-reduce.8.cloned.1.call-done = (f32[768,3,192]{0,2,1:T(8,128)}, f32[192,768]{1,0:T(8,128)}, f32[768,768]{1,0:T(8,128)}, f32[768,768]{1,0:T(8,128)}) async-done(((f32[768,3,192]{0,2,1:T(8,128)}, f32[192,768]{1,0:T(8,128)}, f32[768,768]{1,0:T(8,128)}, f32[768,768]{1,0:T(8,128)}), (f32[768,3,192]{0,2,1:T(8,128)}, f32[192,768]{1,0:T(8,128)}, f32[768,768]{1,0:T(8,128)}, ...) | async-done | bytes 7077904 | tf_op jit(solution)/shard_map/psum | solution.py:219
  460.7 2.9 copy.50
  463.6 0.8 copy.51
  464.4 1.4 copy.52
  465.9 1.1 copy-done.6
  467.0 1.4 copy.53
  (139 shorter events, 2.1 us)
Async XLA Ops:
  7.2 64.5 %copy-start = (bf16[768,768]{1,0:T(8,128)(2,1)S(1)}, bf16[768,768]{1,0:T(8,128)(2,1)}, u32[]{:S(2)}) copy-start(bf16[768,768]{1,0:T(8,128)(2,1)} %param.23) | copy-start | bytes 3538948
  7.2 47.8 %reduce-scatter.5.cloned.1.call-start = ((), (), s32[]{:S(2)}) async-start(), calls=%async_computation.4 | async-start | bytes 1966080 | tf_op jit(solution)/shard_map/reduce_scatter | solution.py:118
  20.3 1.2 copy-start.10
  20.4 1.9 copy-start.47
  20.6 1.7 copy-start.8
  21.5 1.7 copy-start.1
  21.6 1.7 copy-start.22
  22.3 1.9 copy-start.37
  24.2 1.6 copy-start.12
  24.2 30.8 %copy-start.18 = (bf16[512,192]{0,1:T(8,128)(2,1)S(1)}, bf16[512,192]{0,1:T(8,128)(2,1)}, u32[]{:S(2)}) copy-start(bf16[512,192]{0,1:T(8,128)(2,1)} %param.15) | copy-start | bytes 589828
  24.3 30.8 %copy-start.50 = (f32[192]{0:T(256)S(1)}, f32[192]{0:T(256)}, u32[]{:S(2)}) copy-start(f32[192]{0:T(256)} %param.20) | copy-start | bytes 2308
  25.8 36.1 %copy-start.32 = (f32[192]{0:T(256)S(1)}, f32[192]{0:T(256)}, u32[]{:S(2)}) copy-start(f32[192]{0:T(256)} %param.21) | copy-start | bytes 2308
  25.8 36.1 %copy-start.46 = (f32[192]{0:T(256)S(1)}, f32[192]{0:T(256)}, u32[]{:S(2)}) copy-start(f32[192]{0:T(256)} %param.22) | copy-start | bytes 2308
  25.9 45.9 %copy-start.55 = (f32[768]{0:T(1024)S(1)}, f32[768]{0:T(1024)}, u32[]{:S(2)}) copy-start(f32[768]{0:T(1024)} %param.24) | copy-start | bytes 9220
  25.9 79.1 %reduce-scatter.7.cloned.1.call-start = ((), (), s32[]{:S(2)}) async-start(), calls=%async_computation.5 | async-start | bytes 1966080 | tf_op jit(solution)/shard_map/reduce_scatter | solution.py:131
  71.7 2.9 copy-start.53
  76.6 28.4 %copy-start.52 = (f32[192]{0:T(256)S(1)}, f32[192]{0:T(256)}, u32[]{:S(2)}) copy-start(f32[192]{0:T(256)} %param.26) | copy-start | bytes 2308
  76.6 35.3 %copy-start.15 = (bf16[512,192]{0,1:T(8,128)(2,1)S(1)}, bf16[512,192]{0,1:T(8,128)(2,1)}, u32[]{:S(2)}) copy-start(bf16[512,192]{0,1:T(8,128)(2,1)} %param.29) | copy-start | bytes 589828
  76.6 35.3 %copy-start.34 = (f32[192]{0:T(256)S(1)}, f32[192]{0:T(256)}, u32[]{:S(2)}) copy-start(f32[192]{0:T(256)} %param.27) | copy-start | bytes 2308
  76.7 87.7 %reduce-scatter.9.cloned.1.call-start = ((), (), s32[]{:S(2)}) async-start(), calls=%async_computation.6 | async-start | bytes 1966080 | tf_op jit(solution)/shard_map/reduce_scatter | solution.py:151
  118.4 9.8 %copy-start.54 = (bf16[768,768]{1,0:T(8,128)(2,1)S(1)}, bf16[768,768]{1,0:T(8,128)(2,1)}, u32[]{:S(2)}) copy-start(bf16[768,768]{1,0:T(8,128)(2,1)} %param.25) | copy-start | bytes 3538948
  118.4 9.8 %copy-start.30 = (f32[512]{0:T(512)}, f32[512]{0:T(512)S(1)}, u32[]{:S(2)}) copy-start(f32[512]{0:T(512)S(1)} %broadcast_multiply_fusion.1) | copy-start | bytes 6148
  128.2 4.3 copy-start.4
  135.6 28.8 %copy-start.31 = (f32[512]{0:T(512)S(1)}, f32[512]{0:T(512)}, u32[]{:S(2)}) copy-start(f32[512]{0:T(512)} %copy-done.30) | copy-start | bytes 6148
  135.6 28.8 %copy-start.33 = (f32[192]{0:T(256)S(1)}, f32[192]{0:T(256)}, u32[]{:S(2)}) copy-start(f32[192]{0:T(256)} %param.21) | copy-start | bytes 2308
  135.6 28.8 %copy-start.35 = (f32[192]{0:T(256)S(1)}, f32[192]{0:T(256)}, u32[]{:S(2)}) copy-start(f32[192]{0:T(256)} %param.27) | copy-start | bytes 2308
  135.6 28.8 %copy-start.39 = (f32[512]{0:T(512)S(1)}, f32[512]{0:T(512)}, u32[]{:S(2)}) copy-start(f32[512]{0:T(512)} %get-tuple-element.43) | copy-start | bytes 6148
  135.6 28.8 %copy-start.51 = (f32[192]{0:T(256)S(1)}, f32[192]{0:T(256)}, u32[]{:S(2)}) copy-start(f32[192]{0:T(256)} %param.28) | copy-start | bytes 2308
  135.6 102.8 %reduce-scatter.11.cloned.1.call-start = ((), (), s32[]{:S(2)}) async-start(), calls=%async_computation.7 | async-start | bytes 1966080 | tf_op jit(solution)/shard_map/reduce_scatter | solution.py:203
  172.9 11.8 %copy-start.2 = (f32[3,512,512]{1,2,0:T(8,128)S(1)}, f32[3,512,512]{1,2,0:T(8,128)}, u32[]{:S(2)}) copy-start(f32[3,512,512]{1,2,0:T(8,128)} %copy-done.1) | copy-start | bytes 9437188
  174.3 10.4 %copy-start.9 = (pred[512,512]{0,1:T(8,128)(4,1)S(1)}, pred[512,512]{0,1:T(8,128)(4,1)}, u32[]{:S(2)}) copy-start(pred[512,512]{0,1:T(8,128)(4,1)} %copy-done.8) | copy-start | bytes 786436
  174.3 10.4 %copy-start.38 = (f32[3,512]{1,0:T(4,128)S(1)}, f32[3,512]{1,0:T(4,128)}, u32[]{:S(2)}) copy-start(f32[3,512]{1,0:T(4,128)} %copy-done.37) | copy-start | bytes 18436
  184.7 1.2 copy-start.23
  184.7 1.2 copy-start.48
  185.8 2.9 copy-start.56
  185.9 1.4 copy-start.29
  187.3 1.6 copy-start.17
  188.7 2.2 copy-start.26
  191.0 269.7 %all-reduce.8.cloned.1.call-start = ((), (), s32[]{:S(2)}) async-start(), calls=%async_computation.8 | async-start | bytes 14155776 | tf_op jit(solution)/shard_map/psum | solution.py:219
  191.0 3.7 copy-start.5
  191.0 3.7 copy-start.20
  194.7 2.2 copy-start.14
  196.9 1.2 copy-start.25
  196.9 1.2 copy-start.27
  196.9 1.2 copy-start.57
  460.7 3.0 copy-start.21
  460.7 3.8 copy-start.7
  464.4 2.5 copy-start.6
  (15 other events, 12.4 us)
Sparse Core Ops, SparseCore 0:
  26.0 29.0 reduce-scatter.4
  76.8 28.1 reduce-scatter.6
  135.7 28.6 reduce-scatter.8
  191.1 28.1 reduce-scatter.10
  224.7 235.8 all-reduce.7
where the time goes:
time: 476 us; the launch traced here: 475 us
  waiting for transfers between devices  307 us (64%)
  blocking collectives  98.2 us (21%)
  matrix products  32.3 us (7%)
  between operations  14.3 us (3%)
  local copies, waits for them, and re-layouts  12.8 us (3%)
  other arithmetic  10.5 us (2%)
    psum x1, waiting for transfers between devices, per_device(): lax.psum((triple_grad, query_value_grad, output_weight_grad, output_bias_...  220 us
    psum x1, blocking collectives, per_device(): lax.psum((triple_grad, query_value_grad, output_weight_grad, output_bias_...  37.6 us
    all_gather x4, blocking collectives, widen(): return lax.all_gather(piece, 'tensor', axis=1, tiled=True)  37.1 us
    reduce_scatter x1, waiting for transfers between devices, per_device(): lax.psum_scatter(jnp.dot(context_flat, output_weight, preferred_element_t...  29.1 us
    reduce_scatter x1, waiting for transfers between devices, per_device(): lax.psum_scatter(wide_dot(act_half, expand_weight), 'tensor', scatter_dim...  28.7 us
    reduce_scatter x1, waiting for transfers between devices, per_device(): lax.psum_scatter(jnp.dot(activated, reduce_weight, preferred_element_type...  28.3 us
    psum x4, blocking collectives, row_stats(): return lax.psum((jnp.sum(first, axis=1), jnp.sum(second, axis=1)), 'tensor')  23.5 us
    unnamed x120, local copies, waits for them, and re-layouts  11.6 us
  transfers between devices with their start and end apart: 5, of which 4 were waited for; matrix products, arithmetic and copies ran while one was open for 2% of the time, Pallas kernels for 0%

commit v1 on v0

--- a/solution.py
+++ b/solution.py
@@ -1,3 +1,4 @@
+import functools
 import jax
 import jax.numpy as jnp
 from jax import lax
@@ -8,6 +9,34 @@
 EPS = 1e-06
 
 
+def order_slabs(chunk, axis_key):
+    v_now = lax.axis_size(axis_key)
+    clean = lax.axis_index(axis_key)
+    aux, near, heard = (v_now, clean, chunk.shape[1])
+    line_up = []
+    for at in range(aux):
+        line_up.append((at, (at + 1) % aux))
+    crops = []
+    for at in range(aux):
+        crops.append((at, (at - 1) % aux))
+    s_next = jnp.zeros((*chunk.shape[:1], aux * heard, *chunk.shape[2:]), chunk.dtype)
+    s_next = lax.dynamic_update_slice_in_dim(s_next, chunk, near * heard, axis=1)
+    moved = outer = chunk
+    everything = aux // 2
+    for it in range(1, everything + 1):
+        moved = lax.ppermute(moved, axis_name=axis_key, perm=line_up)
+        s_next = lax.dynamic_update_slice_in_dim(s_next, moved, (near - it) % aux * heard, axis=1)
+        if it < aux - everything:
+            outer = lax.ppermute(outer, axis_name=axis_key, perm=crops)
+            s_next = lax.dynamic_update_slice_in_dim(
+                s_next, outer, (near + it) % aux * heard, axis=1
+            )
+    return s_next
+
+
+_link_squares = functools.partial(order_slabs, axis_key="tensor")
+
+
 def gelu_value(pre_act):
     return 0.5 * pre_act * (1.0 + lax.erf(pre_act * 0.7071067811865476))
 
@@ -20,7 +49,7 @@
 
 
 def widen(piece):
-    return lax.all_gather(piece, "tensor", axis=1, tiled=True)
+    return _link_squares(piece)
 
 
 def row_stats(first, second):

time: 476 us -> 549 us (1.15)
  local copies, waits for them, and re-layouts: 12.8 us -> 86.8 us
  blocking collectives: 98.2 us -> 61.4 us
  waiting for transfers between devices: 307 us -> 325 us
  starting transfers between devices: 0.2 us -> 11.6 us
  other arithmetic: 10.5 us -> 16.2 us
    dynamic_update_slice x0 -> x16, local copies, waits for them, and re-layouts: none -> 48.5 us  [the longest x8 21.7 us: order_slabs(): lax.dynamic_update_slice_in_dim(s_next, moved, (near - it) % aux * heard,...]
    all_gather x4 -> x0, blocking collectives: 37.1 us -> none  [widen(): return lax.all_gather(piece, 'tensor', axis=1, tiled=True)]
    ppermute x0 -> x12, local copies, waits for them, and re-layouts: none -> 17.1 us  [the longest x8 11.4 us: order_slabs(): moved = lax.ppermute(moved, axis_name=axis_key, perm=line_up)]
    ppermute x0 -> x12, starting transfers between devices: none -> 11.4 us  [the longest x4 7.25 us: order_slabs(): outer = lax.ppermute(outer, axis_name=axis_key, perm=crops)]
    ppermute x0 -> x12, waiting for transfers between devices: none -> 11.2 us  [the longest x8 11.2 us: order_slabs(): moved = lax.ppermute(moved, axis_name=axis_key, perm=line_up)]
    unnamed x120 -> x109, local copies, waits for them, and re-layouts: 11.6 us -> 14.4 us
  transfers between devices with their start and end apart: 5 -> 17, of which waited for: 4 -> 7; matrix products, arithmetic and copies ran while one was open for 2% -> 13% of each run, Pallas kernels for 0% -> 0%
where the time goes in v1:
time: 549 us; the launch traced here: 547 us
  waiting for transfers between devices  325 us (59%)
  local copies, waits for them, and re-layouts  86.8 us (16%)
  blocking collectives  61.4 us (11%)
  matrix products  31.1 us (6%)
  other arithmetic  16.2 us (3%)
  between operations  14.6 us (3%)
  starting transfers between devices  11.6 us (2%)
    psum x1, waiting for transfers between devices, per_device(): lax.psum((triple_grad, query_value_grad, output_weight_grad, output_bias_...  223 us
    psum x1, blocking collectives, per_device(): lax.psum((triple_grad, query_value_grad, output_weight_grad, output_bias_...  37 us
    reduce_scatter x1, waiting for transfers between devices, per_device(): lax.psum_scatter(wide_dot(act_half, expand_weight), 'tensor', scatter_dim...  30.4 us
    reduce_scatter x1, waiting for transfers between devices, per_device(): lax.psum_scatter(jnp.dot(activated, reduce_weight, preferred_element_type...  30.3 us
    reduce_scatter x1, waiting for transfers between devices, per_device(): lax.psum_scatter(jnp.dot(context_flat, output_weight, preferred_element_t...  29.9 us
    psum x4, blocking collectives, row_stats(): return lax.psum((jnp.sum(first, axis=1), jnp.sum(second, axis=1)), 'tensor')  24.4 us
    dynamic_update_slice x8, local copies, waits for them, and re-layouts, order_slabs(): lax.dynamic_update_slice_in_dim(s_next, moved, (near - it) % aux * heard,...  21.7 us
    dynamic_update_slice x4, local copies, waits for them, and re-layouts, order_slabs(): lax.dynamic_update_slice_in_dim(s_next, outer, (near + it) % aux * heard,...  14.5 us
  transfers between devices with their start and end apart: 17, of which 7 were waited for; matrix products, arithmetic and copies ran while one was open for 13% of the time, Pallas kernels for 0%

profile of v1, /device:TPU:0, one launch (start us, length us, event | category | flops | bytes accessed | tf_op | source)
XLA Modules:
  0.0 547.0 jit_solution(9334502444410470658)
XLA Ops:
  7.8 2.0 collective-permute-start.1
  11.9 2.6 dynamic_update_slice.48
  17.4 2.4 dynamic_update_slice.49
  20.8 3.3 dynamic_update_slice.50
  25.2 1.8 dynamic_update_slice.51
  33.6 29.9 %reduce-scatter.5.cloned.1.call-done = f32[512,192]{0,1:T(8,128)} async-done(((f32[512,768]{0,1:T(8,128)}), f32[512,192]{0,1:T(8,128)}) %reduce-scatter.5.cloned.1.call-update) | async-done | bytes 393232 | tf_op jit(solution)/shard_map/reduce_scatter | solution.py:147
  64.6 5.8 %all-reduce.5 = (f32[512]{0:T(512)S(1)}, f32[512]{0:T(512)S(1)}) all-reduce(f32[512]{0:T(512)S(1)} %get-tuple-element.23, f32[512]{0:T(512)S(1)} %get-tuple-element.22), channel_id=1, replica_groups=mesh['dp'=8,'tensor'=4] {'tensor'}, use_global_device_ids=true, to_apply=%region_6.7 | all-reduce | flops 1024 | bytes 8192 | tf_op jit(solution)/shard_map/psum | solution.py:56
  73.0 3.8 collective-permute-done.3
  78.5 2.6 dynamic_update_slice.52
  82.2 2.4 dynamic_update_slice.53
  85.7 3.3 dynamic_update_slice.54
  90.1 1.8 dynamic_update_slice.55
  91.9 2.0 multiply_convert_fusion.1
  94.8 2.0 fusion.36
  96.8 30.3 %reduce-scatter.7.cloned.1.call-done = f32[512,192]{0,1:T(8,128)} async-done(((f32[512,768]{0,1:T(8,128)}), f32[512,192]{0,1:T(8,128)}) %reduce-scatter.7.cloned.1.call-update) | async-done | bytes 393232 | tf_op jit(solution)/shard_map/reduce_scatter | solution.py:160
  128.9 6.4 %all-reduce.4 = (f32[512]{0:T(512)}, f32[512]{0:T(512)}) all-reduce(f32[512]{0:T(512)} %get-tuple-element.21, f32[512]{0:T(512)S(1)} %get-tuple-element.20), channel_id=1, replica_groups=mesh['dp'=8,'tensor'=4] {'tensor'}, use_global_device_ids=true, to_apply=%region_11.12 | all-reduce | flops 1024 | bytes 8192 | tf_op jit(solution)/shard_map/psum | solution.py:56
  137.7 6.3 %all-reduce.3 = (f32[512]{0:T(512)}, f32[512]{0:T(512)}) all-reduce(f32[512]{0:T(512)} %get-tuple-element.25, f32[512]{0:T(512)} %get-tuple-element.24), channel_id=1, replica_groups=mesh['dp'=8,'tensor'=4] {'tensor'}, use_global_device_ids=true, to_apply=%region_15.16 | all-reduce | flops 1024 | bytes 8192 | tf_op jit(solution)/shard_map/psum | solution.py:56
  145.3 1.8 fusion.25
  148.8 3.7 collective-permute-done.6
  156.2 3.4 dynamic_update_slice.56
  161.4 3.2 dynamic_update_slice.57
  164.7 1.8 copy.40
  166.4 3.8 dynamic_update_slice.58
  170.2 1.8 copy.41
  172.0 3.4 dynamic_update_slice.59
  175.4 3.7 fusion.33
  179.9 2.0 fusion.17
  182.0 30.4 %reduce-scatter.9.cloned.1.call-done = f32[512,192]{0,1:T(8,128)} async-done(((f32[512,768]{0,1:T(8,128)}), f32[512,192]{0,1:T(8,128)}) %reduce-scatter.9.cloned.1.call-update) | async-done | bytes 393232 | tf_op jit(solution)/shard_map/reduce_scatter | solution.py:180
  212.4 2.8 fusion.13
  215.2 5.9 %all-reduce.2 = (f32[512]{0:T(512)S(1)}, f32[512]{0:T(512)S(1)}) all-reduce(f32[512]{0:T(512)} %get-tuple-element.58, f32[512]{0:T(512)} %get-tuple-element.57), channel_id=1, replica_groups=mesh['dp'=8,'tensor'=4] {'tensor'}, use_global_device_ids=true, to_apply=%region_20.21 | all-reduce | flops 1024 | bytes 8192 | tf_op jit(solution)/shard_map/psum | solution.py:56
  224.8 3.8 collective-permute-done.9
  229.2 1.8 copy.42
  231.1 3.6 dynamic_update_slice.60
  234.7 1.8 copy.43
  236.5 3.6 dynamic_update_slice.61
  240.1 1.8 copy.44
  241.9 4.1 dynamic_update_slice.62
  246.0 1.8 copy.45
  247.8 3.1 dynamic_update_slice.63
  252.4 3.1 fusion.32
  259.1 2.0 convolution_bitcast_fusion
  261.2 3.5 fusion.15
  264.7 2.2 fusion.38
  268.1 1.8 fusion.39
  270.7 37.0 %all-reduce = (f32[2,192]{1,0:T(2,128)}, f32[192]{0:T(256)}, f32[192]{0:T(256)}, f32[192]{0:T(256)}, f32[768]{0:T(1024)}, /*index=5*/f32[192]{0:T(256)}, f32[192]{0:T(256)}, f32[192]{0:T(256)}) all-reduce(f32[2,192]{1,0:T(2,128)S(1)} %pad_maximum_fusion.1, f32[192]{0:T(256)S(1)} %get-tuple-element.49, ...), channel_id=1, replica_groups=mesh['dp'=8,'tensor'=4] {'dp'}, use_global_device_ids=true, to_apply=%region_25.26 | all-reduce | flops 2304 | bytes 18432 | tf_op jit(solution)/shard_map/psum | solution.py:248
  307.8 1.8 add.228
  309.6 223.2 %all-reduce.8.cloned.1.call-done = (f32[768,3,192]{0,2,1:T(8,128)}, f32[192,768]{1,0:T(8,128)}, f32[768,768]{1,0:T(8,128)}, f32[768,768]{1,0:T(8,128)}) async-done(((f32[768,3,192]{0,2,1:T(8,128)}, f32[192,768]{1,0:T(8,128)}, f32[768,768]{1,0:T(8,128)}, f32[768,768]{1,0:T(8,128)}), (f32[768,3,192]{0,2,1:T(8,128)}, f32[192,768]{1,0:T(8,128)}, f32[768,768]{1,0:T(8,128)}, ...) | async-done | bytes 7077904 | tf_op jit(solution)/shard_map/psum | solution.py:248
  532.8 2.9 copy.82
  (184 shorter events, 53.3 us)
Async XLA Ops:
  7.2 84.7 %copy-start = (bf16[768,768]{1,0:T(8,128)(2,1)S(1)}, bf16[768,768]{1,0:T(8,128)(2,1)}, u32[]{:S(2)}) copy-start(bf16[768,768]{1,0:T(8,128)(2,1)} %param.23) | copy-start | bytes 3538948
  7.2 8.7 %copy-start.37 = (s32[1,512]{1,0:T(1,128)S(1)}, s32[1,512]{1,0:T(1,128)}, u32[]{:S(2)}) copy-start(s32[1,512]{1,0:T(1,128)} %param.16) | copy-start | bytes 6148
  7.2 56.3 %reduce-scatter.5.cloned.1.call-start = ((), (), s32[]{:S(2)}) async-start(), calls=%async_computation.4 | async-start | bytes 1966080 | tf_op jit(solution)/shard_map/reduce_scatter | solution.py:147
  7.2 7.3 %collective-permute-start = (bf16[512,192]{0,1:T(8,128)(2,1)}, bf16[512,192]{0,1:T(8,128)(2,1)}, u32[]{:S(2)}, u32[]{:S(2)}) collective-permute-start(bf16[512,192]{0,1:T(8,128)(2,1)} %param.15), channel_id=1, source_target_pairs={{0,1},{1,2},{2,3},{3,0},{4,5},{5,6},{6,7},{7,4},{8,9},{9,10},{10,1... | collective-permute-start | bytes 589832 | tf_op jit(solution)/shard_map/ppermute | solution.py:27
  7.8 12.0 %collective-permute-start.1 = (bf16[512,192]{0,1:T(8,128)(2,1)}, bf16[512,192]{0,1:T(8,128)(2,1)}, u32[]{:S(2)}, u32[]{:S(2)}) collective-permute-start(bf16[512,192]{0,1:T(8,128)(2,1)} %param.15), channel_id=1, source_target_pairs={{0,3},{1,0},{2,1},{3,2},{4,7},{5,4},{6,5},{7,6},{8,11},{9,8},{10,9... | collective-permute-start | bytes 589832 | tf_op jit(solution)/shard_map/ppermute | solution.py:30
  11.8 17.6 %copy-start.47 = (f32[3,64]{1,0:T(4,128)}, f32[3,64]{1,0:T(4,128)S(1)}, u32[]{:S(2)}) copy-start(f32[3,64]{1,0:T(4,128)S(1)} %add.204) | copy-start | bytes 2308
  11.9 15.9 %copy-start.33 = (f32[3,64]{1,0:T(4,128)}, f32[3,64]{1,0:T(4,128)S(1)}, u32[]{:S(2)}) copy-start(f32[3,64]{1,0:T(4,128)S(1)} %add.207) | copy-start | bytes 2308
  14.6 9.6 %collective-permute-start.2 = (bf16[512,192]{0,1:T(8,128)(2,1)}, bf16[512,192]{0,1:T(8,128)(2,1)}, u32[]{:S(2)}, u32[]{:S(2)}) collective-permute-start(bf16[512,192]{0,1:T(8,128)(2,1)} %collective-permute-done), channel_id=1, source_target_pairs={{0,1},{1,2},{2,3},{3,0},{4,5},{5,6},{6,7},{7,4},{8,9},{9,10},{10,1... | collective-permute-start | bytes 589832 | tf_op jit(solution)/shard_map/ppermute | solution.py:27
  15.9 11.1 %copy-start.20 = (bf16[768,3,192]{0,2,1:T(8,128)(2,1)S(1)}, bf16[768,3,192]{0,2,1:T(8,128)(2,1)}, u32[]{:S(2)}) copy-start(bf16[768,3,192]{0,2,1:T(8,128)(2,1)} %param.17) | copy-start | bytes 2654212
  16.2 13.2 %copy-start.10 = (pred[512,512]{0,1:T(8,128)(4,1)}, pred[512,512]{0,1:T(8,128)(4,1)S(1)}, u32[]{:S(2)}) copy-start(pred[512,512]{0,1:T(8,128)(4,1)S(1)} %broadcast_compare_fusion) | copy-start | bytes 786436
  31.9 31.6 %copy-start.26 = (bf16[512,192]{0,1:T(8,128)(2,1)S(1)}, bf16[512,192]{0,1:T(8,128)(2,1)}, u32[]{:S(2)}) copy-start(bf16[512,192]{0,1:T(8,128)(2,1)} %param.15) | copy-start | bytes 589828
  31.9 31.6 %copy-start.49 = (f32[192]{0:T(256)S(1)}, f32[192]{0:T(256)}, u32[]{:S(2)}) copy-start(f32[192]{0:T(256)} %param.20) | copy-start | bytes 2308
  33.5 36.9 %copy-start.36 = (f32[192]{0:T(256)S(1)}, f32[192]{0:T(256)}, u32[]{:S(2)}) copy-start(f32[192]{0:T(256)} %param.21) | copy-start | bytes 2308
  33.5 36.9 %copy-start.46 = (f32[192]{0:T(256)S(1)}, f32[192]{0:T(256)}, u32[]{:S(2)}) copy-start(f32[192]{0:T(256)} %param.22) | copy-start | bytes 2308
  33.5 93.6 %reduce-scatter.7.cloned.1.call-start = ((), (), s32[]{:S(2)}) async-start(), calls=%async_computation.5 | async-start | bytes 1966080 | tf_op jit(solution)/shard_map/reduce_scatter | solution.py:160
  71.2 5.5 %collective-permute-start.3 = (bf16[512,192]{0,1:T(8,128)(2,1)}, bf16[512,192]{0,1:T(8,128)(2,1)}, u32[]{:S(2)}, u32[]{:S(2)}) collective-permute-start(bf16[512,192]{0,1:T(8,128)(2,1)} %fusion.19), channel_id=1, source_target_pairs={{0,1},{1,2},{2,3},{3,0},{4,5},{5,6},{6,7},{7,4},{8,9},{9,10},{10,1... | collective-permute-start | bytes 589832 | tf_op jit(solution)/shard_map/ppermute | solution.py:27
  71.2 13.4 %collective-permute-start.4 = (bf16[512,192]{0,1:T(8,128)(2,1)}, bf16[512,192]{0,1:T(8,128)(2,1)}, u32[]{:S(2)}, u32[]{:S(2)}) collective-permute-start(bf16[512,192]{0,1:T(8,128)(2,1)} %fusion.19), channel_id=1, source_target_pairs={{0,3},{1,0},{2,1},{3,2},{4,7},{5,4},{6,5},{7,6},{8,11},{9,8},{10,9... | collective-permute-start | bytes 589832 | tf_op jit(solution)/shard_map/ppermute | solution.py:30
  76.8 12.2 %collective-permute-start.5 = (bf16[512,192]{0,1:T(8,128)(2,1)}, bf16[512,192]{0,1:T(8,128)(2,1)}, u32[]{:S(2)}, u32[]{:S(2)}) collective-permute-start(bf16[512,192]{0,1:T(8,128)(2,1)} %collective-permute-done.3), channel_id=1, source_target_pairs={{0,1},{1,2},{2,3},{3,0},{4,5},{5,6},{6,7},{7,4},{8,9},{9,10},{10,1... | collective-permute-start | bytes 589832 | tf_op jit(solution)/shard_map/ppermute | solution.py:27
  81.1 10.7 %copy-start.51 = (f32[768]{0:T(1024)S(1)}, f32[768]{0:T(1024)}, u32[]{:S(2)}) copy-start(f32[768]{0:T(1024)} %param.24) | copy-start | bytes 9220
  91.9 2.9 copy-start.50
  96.8 115.6 %reduce-scatter.9.cloned.1.call-start = ((), (), s32[]{:S(2)}) async-start(), calls=%async_computation.6 | async-start | bytes 1966080 | tf_op jit(solution)/shard_map/reduce_scatter | solution.py:180
  147.0 5.4 collective-permute-start.6
  147.1 17.6 %collective-permute-start.7 = (bf16[512,192]{0,1:T(8,128)(2,1)}, bf16[512,192]{0,1:T(8,128)(2,1)}, u32[]{:S(2)}, u32[]{:S(2)}) collective-permute-start(bf16[512,192]{0,1:T(8,128)(2,1)} %fusion.25), channel_id=1, source_target_pairs={{0,3},{1,0},{2,1},{3,2},{4,7},{5,4},{6,5},{7,6},{8,11},{9,8},{10,9... | collective-permute-start | bytes 589832 | tf_op jit(solution)/shard_map/ppermute | solution.py:30
  152.5 17.8 %collective-permute-start.8 = (bf16[512,192]{0,1:T(8,128)(2,1)}, bf16[512,192]{0,1:T(8,128)(2,1)}, u32[]{:S(2)}, u32[]{:S(2)}) collective-permute-start(bf16[512,192]{0,1:T(8,128)(2,1)} %collective-permute-done.6), channel_id=1, source_target_pairs={{0,1},{1,2},{2,3},{3,0},{4,5},{5,6},{6,7},{7,4},{8,9},{9,10},{10,1... | collective-permute-start | bytes 589832 | tf_op jit(solution)/shard_map/ppermute | solution.py:27
  181.9 125.8 %reduce-scatter.11.cloned.1.call-start = ((), (), s32[]{:S(2)}) async-start(), calls=%async_computation.7 | async-start | bytes 1966080 | tf_op jit(solution)/shard_map/reduce_scatter | solution.py:232
  222.3 6.9 %copy-start.5 = (f32[512,192]{0,1:T(8,128)}, f32[512,192]{0,1:T(8,128)S(1)}, u32[]{:S(2)}) copy-start(f32[512,192]{0,1:T(8,128)S(1)} %get-tuple-element.50) | copy-start | bytes 1179652
  223.1 5.5 %collective-permute-start.9 = (bf16[512,192]{0,1:T(8,128)(2,1)}, bf16[512,192]{0,1:T(8,128)(2,1)}, u32[]{:S(2)}, u32[]{:S(2)}) collective-permute-start(bf16[512,192]{0,1:T(8,128)(2,1)} %convert_element_type.69), channel_id=1, source_target_pairs={{0,1},{1,2},{2,3},{3,0},{4,5},{5,6},{6,7},{7,4},{8,9},{9,10},{10,1... | collective-permute-start | bytes 589832 | tf_op jit(solution)/shard_map/ppermute | solution.py:27
  223.1 17.0 %collective-permute-start.10 = (bf16[512,192]{0,1:T(8,128)(2,1)}, bf16[512,192]{0,1:T(8,128)(2,1)}, u32[]{:S(2)}, u32[]{:S(2)}) collective-permute-start(bf16[512,192]{0,1:T(8,128)(2,1)} %convert_element_type.69), channel_id=1, source_target_pairs={{0,3},{1,0},{2,1},{3,2},{4,7},{5,4},{6,5},{7,6},{8,11},{9,8},{10,9... | collective-permute-start | bytes 589832 | tf_op jit(solution)/shard_map/ppermute | solution.py:30
  228.6 17.4 %collective-permute-start.11 = (bf16[512,192]{0,1:T(8,128)(2,1)}, bf16[512,192]{0,1:T(8,128)(2,1)}, u32[]{:S(2)}, u32[]{:S(2)}) collective-permute-start(bf16[512,192]{0,1:T(8,128)(2,1)} %collective-permute-done.9), channel_id=1, source_target_pairs={{0,1},{1,2},{2,3},{3,0},{4,5},{5,6},{6,7},{7,4},{8,9},{9,10},{10,1... | collective-permute-start | bytes 589832 | tf_op jit(solution)/shard_map/ppermute | solution.py:27
  240.1 12.2 %copy-start.39 = (f32[3,512]{1,0:T(4,128)S(1)}, f32[3,512]{1,0:T(4,128)}, u32[]{:S(2)}) copy-start(f32[3,512]{1,0:T(4,128)} %copy-done.38) | copy-start | bytes 18436
  252.3 3.1 copy-start.17
  252.3 3.2 copy-start.2
  252.3 3.2 copy-start.11
  252.3 3.2 copy-start.30
  252.3 3.2 copy-start.48
  255.4 2.9 copy-start.31
  257.0 2.1 copy-start.21
  261.1 271.7 %all-reduce.8.cloned.1.call-start = ((), (), s32[]{:S(2)}) async-start(), calls=%async_computation.8 | async-start | bytes 14155776 | tf_op jit(solution)/shard_map/psum | solution.py:248
  261.1 3.5 copy-start.7
  261.1 3.5 copy-start.13
  264.6 2.2 copy-start.23
  264.6 2.2 copy-start.25
  264.6 2.2 copy-start.32
  264.6 2.3 copy-start.18
  270.0 37.8 %copy-start.6 = (f32[512,192]{0,1:T(8,128)S(1)}, f32[512,192]{0,1:T(8,128)}, u32[]{:S(2)}) copy-start(f32[512,192]{0,1:T(8,128)} %copy-done.5) | copy-start | bytes 1179652
  532.8 3.0 copy-start.28
  532.8 3.8 copy-start.9
  536.6 2.5 copy-start.8
  (21 other events, 21.1 us)
Sparse Core Ops, SparseCore 0:
  33.7 29.7 reduce-scatter.4
  96.9 30.1 reduce-scatter.6
  182.0 30.2 reduce-scatter.8
  261.2 30.1 reduce-scatter.10
  296.8 235.8 all-reduce.7
